TPU v7x, 512 devices: a whole 4x4x16 slice. The times are simulated.
512 devices in a mesh: tile: 32 (over z, core), band: 4 (over x), pos: 4 (over y).
Axes of the slice: x: 4, y: 4, z: 16, core: 2. Of those that a mesh axis runs over, the one named last changes fastest.
Arguments:
- object_planes: float32 [2, 8192, 1024], P(None, 'tile', 'band'), may hold values from -6 to 6
- probe_planes: float32 [2, 2, 256, 256], replicated, may hold values from -6 to 6
- patterns: float32 [32, 4, 4, 3, 256, 256], P('tile', 'band', 'pos'), may hold values from 0.5 to 8
- offsets: int32 [32, 4, 4, 3, 2], P('tile', 'band', 'pos'), may hold values from 0 to 255, as said below
- counts: int32 [32, 4, 4], P('tile', 'band', 'pos'), may hold values from 0 to 3, as said below
Outputs:
- object_new: float32 [2, 8192, 1024], P(None, 'tile', 'band')
- probe_new: float32 [2, 2, 256, 256], replicated
Inputs may be any that keep to these rules, and one draw needn't show every extreme that they name: `offsets`: corners lie inside their tile: rows below 256, columns below 256. Only the first counts[t, b, p] slots of a device hold positions; later slots are to be ignored. `counts`: each device holds at most 3 positions; in every tile one device along pos holds exactly 3, and the 4 devices of a tile hold exactly 8 positions together.
All inputs are finite; a program needn't handle non-finite values.
Results may differ from a plain program's by a relative error of at most 0.0003.
Values sent between devices are 32-bit elements; how exact they have to be, the bound alone decides.
No kernel may reach another device: no remote copies, remote signals or barrier semaphores. Data moves between devices by JAX's collectives and lax.ppermute only.
A program may use at most 192 MiB of HBM per device.

v0:
```python
import math
import jax
import jax.numpy as jnp
from jax import lax
from jax.sharding import PartitionSpec as P

precise = lax.Precision.HIGHEST


def shifted(block, axis, distance):
    devices = range(lax.axis_size(axis))
    route = [(i - distance, i) for i in devices if i - distance in devices]
    return lax.ppermute(block, axis, route)


def dft_tables(pixels):
    indices = jnp.arange(pixels, dtype=jnp.int32)
    phase = indices[:, None] * indices[None, :] % pixels
    angle = phase.astype(jnp.float32) * (2.0 * math.pi / pixels)
    factor = 1.0 / math.sqrt(pixels)
    return (jnp.cos(angle) * factor, jnp.sin(angle) * factor)


def transform(real_part, imag_part, cosine, sine_table, direction):
    left_real = jnp.einsum(
        "ij,nmjk->nmik", cosine, real_part, precision=precise
    ) + direction * jnp.einsum("ij,nmjk->nmik", sine_table, imag_part, precision=precise)
    left_imag = jnp.einsum(
        "ij,nmjk->nmik", cosine, imag_part, precision=precise
    ) - direction * jnp.einsum("ij,nmjk->nmik", sine_table, real_part, precision=precise)
    out_real = jnp.einsum(
        "nmij,jk->nmik", left_real, cosine, precision=precise
    ) + direction * jnp.einsum("nmij,jk->nmik", left_imag, sine_table, precision=precise)
    out_imag = jnp.einsum(
        "nmij,jk->nmik", left_imag, cosine, precision=precise
    ) - direction * jnp.einsum("nmij,jk->nmik", left_real, sine_table, precision=precise)
    return (out_real, out_imag)


def on_device(object_planes, probe_planes, patterns, offsets, counts):
    pixels = probe_planes.shape[-1]
    capacity = patterns.shape[3]
    tile_rows = object_planes.shape[1]
    tile_cols = object_planes.shape[2]
    beside_cols = shifted(object_planes, "band", -1)
    widened = jnp.concatenate([object_planes, beside_cols], axis=2)
    below_rows = shifted(widened, "tile", -1)
    extended = jnp.concatenate([widened, below_rows], axis=1)
    local_count = counts.reshape(())
    frames = patterns[0, 0, 0]
    places = offsets[0, 0, 0]
    weights = (jnp.arange(capacity, dtype=jnp.int32) < local_count).astype(jnp.float32)
    slot_total = frames.shape[0]
    zero_index = jnp.int32(0)
    patches = jnp.stack(
        [
            lax.dynamic_slice(
                extended, (zero_index, places[number, 0], places[number, 1]), (2, pixels, pixels)
            )
            for number in range(slot_total)
        ]
    )
    patch_real = patches[:, 0][:, None]
    patch_imag = patches[:, 1][:, None]
    probe_real = probe_planes[0][None]
    probe_imag = probe_planes[1][None]
    wave_real = probe_real * patch_real - probe_imag * patch_imag
    wave_imag = probe_real * patch_imag + probe_imag * patch_real
    cosine, sine_table = dft_tables(pixels)
    far_real, far_imag = transform(wave_real, wave_imag, cosine, sine_table, 1.0)
    intensity = jnp.sum(far_real * far_real + far_imag * far_imag, axis=1)
    scaling = (jnp.sqrt(frames) / jnp.sqrt(intensity + 1.0))[:, None]
    back_real, back_imag = transform(
        far_real * scaling, far_imag * scaling, cosine, sine_table, -1.0
    )
    corr_real = back_real - wave_real
    corr_imag = back_imag - wave_imag
    slot_weight = weights[:, None, None]
    object_real = slot_weight * jnp.sum(probe_real * corr_real + probe_imag * corr_imag, axis=1)
    object_imag = slot_weight * jnp.sum(probe_real * corr_imag - probe_imag * corr_real, axis=1)
    probe_power = jnp.sum(probe_planes[0] ** 2 + probe_planes[1] ** 2, axis=0)
    lighting = slot_weight * probe_power[None]
    contributions = jnp.stack([object_real, object_imag, lighting], axis=1)
    plane_count = contributions.shape[1]
    running = jnp.zeros((plane_count, tile_rows + pixels, tile_cols + pixels), jnp.float32)
    for number in range(slot_total):
        corner_at = (zero_index, places[number, 0], places[number, 1])
        previous = lax.dynamic_slice(running, corner_at, (plane_count, pixels, pixels))
        running = lax.dynamic_update_slice(running, previous + contributions[number], corner_at)
    mode_weight = weights[:, None, None, None]
    numer_real = jnp.sum(mode_weight * (patch_real * corr_real + patch_imag * corr_imag), axis=0)
    numer_imag = jnp.sum(mode_weight * (patch_real * corr_imag - patch_imag * corr_real), axis=0)
    density = jnp.sum(slot_weight * (patches[:, 0] ** 2 + patches[:, 1] ** 2), axis=0)
    from_left = shifted(running[:, :, tile_cols:], "band", 1)
    column_core = running[:, :, :tile_cols].at[:, :, :pixels].add(from_left)
    from_above = shifted(column_core[:, tile_rows:, :], "tile", 1)
    tile_core = column_core[:, :tile_rows, :].at[:, :pixels, :].add(from_above)
    tile_total = lax.psum(tile_core, "pos")
    tile_light = tile_total[2]
    object_new = object_planes + tile_total[:2] / (tile_light + 1.0)
    sum_numer, sum_density = lax.psum(
        (jnp.stack([numer_real, numer_imag]), density), ("tile", "band", "pos")
    )
    probe_new = probe_planes + sum_numer / (sum_density + 1.0)
    return (object_new, probe_new)


def solution(mesh):
    in_specs = (
        P(None, "tile", "band"),
        P(),
        P("tile", "band", "pos", None, None, None),
        P("tile", "band", "pos", None, None),
        P("tile", "band", "pos"),
    )
    out_specs = (P(None, "tile", "band"), P())
    return jax.shard_map(
        on_device, mesh=mesh, in_specs=in_specs, out_specs=out_specs, check_vma=False
    )
```

profile of v0, /device:TPU:2, one launch (start us, length us, event | category | flops | bytes accessed | tf_op | source)
XLA Modules:
  0.0 733.1 jit_solution(11217168582069033955)
XLA Ops:
  7.2 0.0 copy-start.2
  7.2 0.0 all-reduce.6.cloned.1.call-start
  7.2 8.0 %collective-permute-start = (f32[2,256,256]{2,1,0:T(8,128)}, f32[2,256,256]{2,1,0:T(8,128)S(1)}, u32[]{:S(2)}, u32[]{:S(2)}) collective-permute-start(f32[2,256,256]{2,1,0:T(8,128)} %param.13), channel_id=1, source_target_pairs={{4,0},{8,4},{12,8},{5,1},{9,5},{13,9},{6,2},{10,6},{14,10},{7,3},{... | collective-permute-start | bytes 1572872 | tf_op jit(solution)/shard_map/ppermute | solution.py:13
  15.2 1.1 constant_dynamic-update-slice_fusion.1
  16.3 6.8 collective-permute-done
  23.1 0.1 constant_dynamic-update-slice_fusion
  23.2 1.3 collective-permute-start.1
  24.5 0.6 fusion.170
  37.1 0.1 add_reduce_fusion.2
  37.2 0.1 slice_bitcast_fusion.6
  37.3 0.0 collective-permute-done.1
  37.3 1.0 fusion.63
  38.2 0.1 pad_maximum_fusion.1
  38.4 0.1 slice_bitcast_fusion.4
  38.5 1.0 copy-done
  39.5 3.7 fusion.16
  43.2 3.7 fusion.31
  46.9 4.1 fusion.8
  51.0 3.6 fusion.10
  54.6 3.7 fusion.17
  58.3 3.7 fusion.30
  62.0 3.8 fusion.20
  65.8 0.0 copy-start.7
  65.9 3.8 add_reduce_fusion.1
  69.6 0.3 bitcast_multiply_fusion.2
  69.9 3.6 fusion.36
  73.5 3.8 fusion.32
  77.3 3.6 multiply_subtract_fusion
  80.9 3.6 fusion
  84.6 4.0 fusion.2
  88.6 3.6 multiply_add_fusion
  92.2 3.9 add_subtract_fusion
  96.2 6.0 multiply_reduce_fusion.1
  102.1 0.3 bitcast_multiply_fusion.1
  102.4 0.2 pad_maximum_fusion
  102.6 1.0 slice_bitcast_fusion.2
  103.6 0.7 copy-done.4
  104.3 0.4 broadcast_in_dim.2
  104.7 10.4 %dynamic_update_slice.9 = f32[3,512,512]{2,1,0:T(8,128)S(1)} dynamic-update-slice(f32[3,512,512]{2,1,0:T(8,128)S(1)} %broadcast_in_dim.2, f32[3,256,256]{2,1,0:T(8,128)} %slice_bitcast_fusion.2, s32[]{:T(128)} %constant.88.clone.1, s32[]{:T(128)S(6)} %select_n.65, s32[]{:T(128)S(6)} %select_n.66) | dynamic-update-slice | bytes 1572868 | tf_op jit(solution)/shard_map/dynamic_update_slice | solution.py:89
  115.1 2.3 fusion.39
  117.4 10.9 %dynamic_update_slice.10 = f32[3,512,512]{2,1,0:T(8,128)S(1)} dynamic-update-slice(f32[3,512,512]{2,1,0:T(8,128)S(1)} %dynamic_update_slice.9, f32[3,256,256]{2,1,0:T(8,128)} %fusion.39, s32[]{:T(128)} %constant.88.clone.1, s32[]{:T(128)S(6)} %select_n.67, s32[]{:T(128)S(6)} %select_n.68) | dynamic-update-slice | bytes 1572868 | tf_op jit(solution)/shard_map/dynamic_update_slice | solution.py:89
  128.2 2.3 fusion.38
  130.5 10.2 %dynamic_update_slice.11 = f32[3,512,512]{2,1,0:T(8,128)S(1)} dynamic-update-slice(f32[3,512,512]{2,1,0:T(8,128)S(1)} %dynamic_update_slice.10, f32[3,256,256]{2,1,0:T(8,128)} %fusion.38, s32[]{:T(128)} %constant.88.clone.1, s32[]{:T(128)S(6)} %select_n.69, s32[]{:T(128)S(6)} %select_n.70) | dynamic-update-slice | bytes 1572868 | tf_op jit(solution)/shard_map/dynamic_update_slice | solution.py:89
  140.8 0.2 slice.130
  141.0 7.9 %collective-permute-start.2 = (f32[3,512,256]{2,1,0:T(8,128)S(1)}, f32[3,512,256]{2,1,0:T(8,128)S(1)}, u32[]{:S(2)}, u32[]{:S(2)}) collective-permute-start(f32[3,512,256]{2,1,0:T(8,128)S(1)} %slice.130), channel_id=1, source_target_pairs={{0,4},{4,8},{8,12},{1,5},{5,9},{9,13},{2,6},{6,10},{10,14},{3,7},{... | collective-permute-start | bytes 4718600 | tf_op jit(solution)/shard_map/ppermute | solution.py:13
  148.8 34.4 %collective-permute-done.2 = f32[3,512,256]{2,1,0:T(8,128)S(1)} collective-permute-done((f32[3,512,256]{2,1,0:T(8,128)S(1)}, f32[3,512,256]{2,1,0:T(8,128)S(1)}, u32[]{:S(2)}, u32[]{:S(2)}) %collective-permute-start.2) | collective-permute-done | bytes 1572896 | tf_op jit(solution)/shard_map/ppermute | solution.py:13
  183.2 0.3 slice_add_fusion
  183.5 0.1 slice.132
  183.6 2.7 collective-permute-start.3
  186.3 1.0 pad_maximum_fusion.2
  187.4 0.9 multiply_reduce_fusion.2
  188.2 0.0 all-reduce.6.cloned.1.call-update
  188.3 0.0 copy-start.3
  188.3 0.0 all-reduce.4.cloned.1.call-start
  188.3 0.0 collective-permute-done.3
  188.3 2.2 slice_add_fusion.1
  190.5 0.0 all-reduce.4.cloned.1.call-update
  190.6 472.6 %all-reduce.6.cloned.1.call-done = (f32[2,2,256,256]{3,2,1,0:T(8,128)}, f32[256,256]{1,0:T(8,128)}) async-done(((f32[2,2,256,256]{3,2,1,0:T(8,128)}, f32[256,256]{1,0:T(8,128)}), (f32[2,2,256,256]{3,2,1,0:T(8,128)}, f32[256,256]{1,0:T(8,128)})) %all-reduce.6.cloned.1.call-update) | async-done | bytes 1310736 | tf_op jit(solution)/shard_map/psum | solution.py:101
  663.2 1.0 broadcast_add_fusion
  664.2 0.0 copy-start.6
  664.2 2.4 divide_add_fusion
  666.6 56.5 %all-reduce.4.cloned.1.call-done = f32[3,256,256]{2,1,0:T(8,128)} async-done(((f32[3,256,256]{2,1,0:T(8,128)}), f32[3,256,256]{2,1,0:T(8,128)}) %all-reduce.4.cloned.1.call-update) | async-done | bytes 786448 | tf_op jit(solution)/shard_map/psum | solution.py:98
  723.1 1.0 fusion.70
  724.1 1.9 fusion.66
  (17 shorter events, 0.0 us)
Async XLA Ops:
  7.2 17.3 %copy-start.10 = (s32[1,1,1,3,2]{3,4,2,1,0:T(2,128)S(1)}, s32[1,1,1,3,2]{3,4,2,1,0:T(2,128)}, u32[]{:S(2)}) copy-start(s32[1,1,1,3,2]{3,4,2,1,0:T(2,128)} %param.16) | copy-start | bytes 76
  7.2 29.9 %copy-start.2 = (f32[2,2,256,256]{3,2,1,0:T(8,128)S(1)}, f32[2,2,256,256]{3,2,1,0:T(8,128)}, u32[]{:S(2)}) copy-start(f32[2,2,256,256]{3,2,1,0:T(8,128)} %param.14) | copy-start | bytes 3145732
  7.2 656.0 %all-reduce.6.cloned.1.call-start = ((), (), s32[]{:S(2)}) async-start(), calls=%async_computation.1 | async-start | bytes 2621440 | tf_op jit(solution)/shard_map/psum | solution.py:101
  7.2 15.9 %collective-permute-start = (f32[2,256,256]{2,1,0:T(8,128)}, f32[2,256,256]{2,1,0:T(8,128)S(1)}, u32[]{:S(2)}, u32[]{:S(2)}) collective-permute-start(f32[2,256,256]{2,1,0:T(8,128)} %param.13), channel_id=1, source_target_pairs={{4,0},{8,4},{12,8},{5,1},{9,5},{13,9},{6,2},{10,6},{14,10},{7,3},{... | collective-permute-start | bytes 1572872 | tf_op jit(solution)/shard_map/ppermute | solution.py:13
  23.2 14.1 %collective-permute-start.1 = (f32[2,256,512]{2,1,0:T(8,128)S(1)}, f32[2,256,512]{2,1,0:T(8,128)S(1)}, u32[]{:S(2)}, u32[]{:S(2)}) collective-permute-start(f32[2,256,512]{2,1,0:T(8,128)S(1)} %constant_dynamic-update-slice_fusion), channel_id=1, source_target_pairs={{16,0},{32,16},{48,32},{64,48},{80,64},{96,80},{112,96},{128,112},... | collective-permute-start | bytes 3145736 | tf_op jit(solution)/shard_map/ppermute | solution.py:13
  38.3 1.1 copy-start
  65.8 3.8 copy-start.7
  102.6 1.7 copy-start.4
  141.0 42.3 %collective-permute-start.2 = (f32[3,512,256]{2,1,0:T(8,128)S(1)}, f32[3,512,256]{2,1,0:T(8,128)S(1)}, u32[]{:S(2)}, u32[]{:S(2)}) collective-permute-start(f32[3,512,256]{2,1,0:T(8,128)S(1)} %slice.130), channel_id=1, source_target_pairs={{0,4},{4,8},{8,12},{1,5},{5,9},{9,13},{2,6},{6,10},{10,14},{3,7},{... | collective-permute-start | bytes 4718600 | tf_op jit(solution)/shard_map/ppermute | solution.py:13
  183.2 3.1 copy-start.8
  183.2 3.1 copy-start.9
  183.5 3.9 copy-start.5
  183.5 3.9 copy-start.1
  183.6 4.7 collective-permute-start.3
  188.3 475.9 %copy-start.3 = (f32[2,2,256,256]{3,2,1,0:T(8,128)S(1)}, f32[2,2,256,256]{3,2,1,0:T(8,128)}, u32[]{:S(2)}) copy-start(f32[2,2,256,256]{3,2,1,0:T(8,128)} %param.14) | copy-start | bytes 3145732
  188.3 534.9 %all-reduce.4.cloned.1.call-start = ((), (), s32[]{:S(2)}) async-start(), calls=%async_computation | async-start | bytes 1572864 | tf_op jit(solution)/shard_map/psum | solution.py:98
  664.2 59.9 %copy-start.6 = (f32[2,256,256]{2,1,0:T(8,128)S(1)}, f32[2,256,256]{2,1,0:T(8,128)}, u32[]{:S(2)}) copy-start(f32[2,256,256]{2,1,0:T(8,128)} %param.13) | copy-start | bytes 1572868
Sparse Core Ops, SparseCore 0:
  188.4 474.7 all-reduce.5
  665.6 57.5 all-reduce.3
where the time goes:
time: 743 us; the launch traced here: 733 us
  waiting for transfers between devices  570 us (77%)
  matrix products  62.2 us (8%)
  local copies, waits for them, and re-layouts  36.8 us (5%)
  between operations  26.6 us (4%)
  starting transfers between devices  19.9 us (3%)
  other arithmetic  17.1 us (2%)
    psum x1, waiting for transfers between devices, on_device(): lax.psum((jnp.stack([numer_real, numer_imag]), density), ('tile', 'band',...  473 us
    psum x1, waiting for transfers between devices, on_device(): tile_total = lax.psum(tile_core, 'pos')  56.5 us
    ppermute x4, waiting for transfers between devices, shifted(): return lax.ppermute(block, axis, route)  41.2 us
    dynamic_update_slice x3, local copies, waits for them, and re-layouts, on_device(): lax.dynamic_update_slice(running, previous + contributions[number], corne...  31.5 us
    ppermute x4, starting transfers between devices, shifted(): return lax.ppermute(block, axis, route)  19.8 us
  transfers between devices with their start and end apart: 6, of which 4 were waited for; matrix products, arithmetic and copies ran while one was open for 1% of the time, Pallas kernels for 0%

commit v1 on v0

--- a/solution.py
+++ b/solution.py
@@ -95,7 +95,8 @@
     column_core = running[:, :, :tile_cols].at[:, :, :pixels].add(from_left)
     from_above = shifted(column_core[:, tile_rows:, :], "tile", 1)
     tile_core = column_core[:, :tile_rows, :].at[:, :pixels, :].add(from_above)
-    tile_total = lax.psum(tile_core, "pos")
+    blocks = lax.all_gather(tile_core, "pos")
+    tile_total = jnp.sum(blocks, axis=0)
     tile_light = tile_total[2]
     object_new = object_planes + tile_total[:2] / (tile_light + 1.0)
     sum_numer, sum_density = lax.psum(

time: 743 us -> 691 us (0.930)
  the two profiles are of different devices: /device:TPU:2 before, /device:TPU:1 now
where the time goes in v1:
time: 691 us; the launch traced here: 681 us
  waiting for transfers between devices  517 us (75%)
  matrix products  62.2 us (9%)
  local copies, waits for them, and re-layouts  38.5 us (6%)
  between operations  28 us (4%)
  starting transfers between devices  18.6 us (3%)
  other arithmetic  17.2 us (2%)
    psum x1, waiting for transfers between devices, on_device(): lax.psum((jnp.stack([numer_real, numer_imag]), density), ('tile', 'band',...  469 us
    ppermute x4, waiting for transfers between devices, shifted(): return lax.ppermute(block, axis, route)  48.3 us
    dynamic_update_slice x3, local copies, waits for them, and re-layouts, on_device(): lax.dynamic_update_slice(running, previous + contributions[number], corne...  33.2 us
    ppermute x4, starting transfers between devices, shifted(): return lax.ppermute(block, axis, route)  18.5 us
  transfers between devices with their start and end apart: 6, of which 5 were waited for; matrix products, arithmetic and copies ran while one was open for 1% of the time, Pallas kernels for 0%

profile of v1, /device:TPU:1, one launch (start us, length us, event | category | flops | bytes accessed | tf_op | source)
XLA Modules:
  0.0 681.4 jit_solution(3185693564247416034)
XLA Ops:
  8.0 0.0 copy-start.10
  8.0 0.0 copy-start.2
  8.0 0.0 all-reduce.3.cloned.1.call-start
  8.1 1.4 collective-permute-start
  9.5 1.1 constant_dynamic-update-slice_fusion.1
  10.6 8.3 %collective-permute-done = f32[2,256,256]{2,1,0:T(8,128)S(1)} collective-permute-done((f32[2,256,256]{2,1,0:T(8,128)}, f32[2,256,256]{2,1,0:T(8,128)S(1)}, u32[]{:S(2)}, u32[]{:S(2)}) %collective-permute-start) | collective-permute-done | bytes 524320 | tf_op jit(solution)/shard_map/ppermute | solution.py:13
  18.9 0.1 constant_dynamic-update-slice_fusion
  19.0 9.3 %collective-permute-start.1 = (f32[2,256,512]{2,1,0:T(8,128)S(1)}, f32[2,256,512]{2,1,0:T(8,128)S(1)}, u32[]{:S(2)}, u32[]{:S(2)}) collective-permute-start(f32[2,256,512]{2,1,0:T(8,128)S(1)} %constant_dynamic-update-slice_fusion), channel_id=1, source_target_pairs={{16,0},{32,16},{48,32},{64,48},{80,64},{96,80},{112,96},{128,112},... | collective-permute-start | bytes 3145736 | tf_op jit(solution)/shard_map/ppermute | solution.py:13
  28.3 0.6 fusion.170
  41.0 0.1 add_reduce_fusion.2
  41.0 0.1 slice_bitcast_fusion.6
  41.1 0.3 collective-permute-done.1
  41.4 1.0 fusion.63
  42.4 0.1 pad_maximum_fusion.1
  42.5 0.1 slice_bitcast_fusion.4
  42.6 1.0 copy-done
  43.6 3.7 fusion.16
  47.3 3.7 fusion.31
  51.1 4.1 fusion.8
  55.1 3.6 fusion.10
  58.7 3.7 fusion.17
  62.4 3.7 fusion.30
  66.2 3.8 fusion.20
  70.0 0.0 copy-start.7
  70.0 3.8 add_reduce_fusion.1
  73.8 0.3 bitcast_multiply_fusion.2
  74.1 3.6 fusion.36
  77.7 3.8 fusion.32
  81.5 3.6 multiply_subtract_fusion
  85.1 3.6 fusion
  88.7 4.0 fusion.2
  92.7 3.6 multiply_add_fusion
  96.4 3.9 add_subtract_fusion
  100.3 6.0 multiply_reduce_fusion.1
  106.3 0.3 bitcast_multiply_fusion.1
  106.6 0.2 pad_maximum_fusion
  106.7 1.0 slice_bitcast_fusion.2
  107.7 0.7 copy-done.4
  108.4 0.4 broadcast_in_dim.2
  108.8 10.9 %dynamic_update_slice.9 = f32[3,512,512]{2,1,0:T(8,128)S(1)} dynamic-update-slice(f32[3,512,512]{2,1,0:T(8,128)S(1)} %broadcast_in_dim.2, f32[3,256,256]{2,1,0:T(8,128)} %slice_bitcast_fusion.2, s32[]{:T(128)} %constant.88.clone.1, s32[]{:T(128)S(6)} %select_n.65, s32[]{:T(128)S(6)} %select_n.66) | dynamic-update-slice | bytes 1572868 | tf_op jit(solution)/shard_map/dynamic_update_slice | solution.py:89
  119.7 2.3 fusion.39
  122.0 10.2 %dynamic_update_slice.10 = f32[3,512,512]{2,1,0:T(8,128)S(1)} dynamic-update-slice(f32[3,512,512]{2,1,0:T(8,128)S(1)} %dynamic_update_slice.9, f32[3,256,256]{2,1,0:T(8,128)} %fusion.39, s32[]{:T(128)} %constant.88.clone.1, s32[]{:T(128)S(6)} %select_n.67, s32[]{:T(128)S(6)} %select_n.68) | dynamic-update-slice | bytes 1572868 | tf_op jit(solution)/shard_map/dynamic_update_slice | solution.py:89
  132.2 2.3 fusion.38
  134.5 12.1 %dynamic_update_slice.11 = f32[3,512,512]{2,1,0:T(8,128)S(1)} dynamic-update-slice(f32[3,512,512]{2,1,0:T(8,128)S(1)} %dynamic_update_slice.10, f32[3,256,256]{2,1,0:T(8,128)} %fusion.38, s32[]{:T(128)} %constant.88.clone.1, s32[]{:T(128)S(6)} %select_n.69, s32[]{:T(128)S(6)} %select_n.70) | dynamic-update-slice | bytes 1572868 | tf_op jit(solution)/shard_map/dynamic_update_slice | solution.py:89
  146.6 0.2 slice.130
  146.8 1.8 collective-permute-start.2
  148.6 32.8 %collective-permute-done.2 = f32[3,512,256]{2,1,0:T(8,128)S(1)} collective-permute-done((f32[3,512,256]{2,1,0:T(8,128)S(1)}, f32[3,512,256]{2,1,0:T(8,128)S(1)}, u32[]{:S(2)}, u32[]{:S(2)}) %collective-permute-start.2) | collective-permute-done | bytes 1572896 | tf_op jit(solution)/shard_map/ppermute | solution.py:13
  181.3 0.3 slice_add_fusion
  181.6 0.1 slice.132
  181.7 6.0 collective-permute-start.3
  187.7 1.0 pad_maximum_fusion.2
  188.8 0.0 copy-done.1
  188.8 0.9 multiply_reduce_fusion.2
  189.6 0.0 all-reduce.3.cloned.1.call-update
  189.6 0.0 copy-start.3
  189.6 0.0 all-gather.3.cloned.1.call-start
  189.7 6.9 %collective-permute-done.3 = f32[3,256,256]{2,1,0:T(8,128)S(1)} collective-permute-done((f32[3,256,256]{2,1,0:T(8,128)S(1)}, f32[3,256,256]{2,1,0:T(8,128)S(1)}, u32[]{:S(2)}, u32[]{:S(2)}) %collective-permute-start.3) | collective-permute-done | bytes 786464 | tf_op jit(solution)/shard_map/ppermute | solution.py:13
  196.6 2.1 slice_add_fusion.1
  198.7 0.0 all-gather.3.cloned.1.call-update
  198.7 468.5 %all-reduce.3.cloned.1.call-done = (f32[2,2,256,256]{3,2,1,0:T(8,128)}, f32[256,256]{1,0:T(8,128)}) async-done(((f32[2,2,256,256]{3,2,1,0:T(8,128)}, f32[256,256]{1,0:T(8,128)}), (f32[2,2,256,256]{3,2,1,0:T(8,128)}, f32[256,256]{1,0:T(8,128)})) %all-reduce.3.cloned.1.call-update) | async-done | bytes 1310736 | tf_op jit(solution)/shard_map/psum | solution.py:102
  667.2 1.0 broadcast_add_fusion
  668.2 2.4 divide_add_fusion
  670.6 2.2 reduce_sum.82
  672.9 0.9 fusion.66
  (18 shorter events, 0.1 us)
Async XLA Ops:
  8.0 20.3 %copy-start.10 = (s32[1,1,1,3,2]{3,4,2,1,0:T(2,128)S(1)}, s32[1,1,1,3,2]{3,4,2,1,0:T(2,128)}, u32[]{:S(2)}) copy-start(s32[1,1,1,3,2]{3,4,2,1,0:T(2,128)} %param.16) | copy-start | bytes 76
  8.0 32.9 %copy-start.2 = (f32[2,2,256,256]{3,2,1,0:T(8,128)S(1)}, f32[2,2,256,256]{3,2,1,0:T(8,128)}, u32[]{:S(2)}) copy-start(f32[2,2,256,256]{3,2,1,0:T(8,128)} %param.14) | copy-start | bytes 3145732
  8.0 659.2 %all-reduce.3.cloned.1.call-start = ((), (), s32[]{:S(2)}) async-start(), calls=%async_computation.1 | async-start | bytes 2621440 | tf_op jit(solution)/shard_map/psum | solution.py:102
  8.1 10.9 %collective-permute-start = (f32[2,256,256]{2,1,0:T(8,128)}, f32[2,256,256]{2,1,0:T(8,128)S(1)}, u32[]{:S(2)}, u32[]{:S(2)}) collective-permute-start(f32[2,256,256]{2,1,0:T(8,128)} %param.13), channel_id=1, source_target_pairs={{4,0},{8,4},{12,8},{5,1},{9,5},{13,9},{6,2},{10,6},{14,10},{7,3},{... | collective-permute-start | bytes 1572872 | tf_op jit(solution)/shard_map/ppermute | solution.py:13
  19.0 22.5 %collective-permute-start.1 = (f32[2,256,512]{2,1,0:T(8,128)S(1)}, f32[2,256,512]{2,1,0:T(8,128)S(1)}, u32[]{:S(2)}, u32[]{:S(2)}) collective-permute-start(f32[2,256,512]{2,1,0:T(8,128)S(1)} %constant_dynamic-update-slice_fusion), channel_id=1, source_target_pairs={{16,0},{32,16},{48,32},{64,48},{80,64},{96,80},{112,96},{128,112},... | collective-permute-start | bytes 3145736 | tf_op jit(solution)/shard_map/ppermute | solution.py:13
  42.5 1.1 copy-start
  70.0 3.8 copy-start.7
  106.7 1.7 copy-start.4
  146.8 34.5 %collective-permute-start.2 = (f32[3,512,256]{2,1,0:T(8,128)S(1)}, f32[3,512,256]{2,1,0:T(8,128)S(1)}, u32[]{:S(2)}, u32[]{:S(2)}) collective-permute-start(f32[3,512,256]{2,1,0:T(8,128)S(1)} %slice.130), channel_id=1, source_target_pairs={{0,4},{4,8},{8,12},{1,5},{5,9},{9,13},{2,6},{6,10},{10,14},{3,7},{... | collective-permute-start | bytes 4718600 | tf_op jit(solution)/shard_map/ppermute | solution.py:13
  181.3 6.4 copy-start.8
  181.3 6.4 copy-start.9
  181.6 7.1 %copy-start.5 = (f32[3,512,256]{2,1,0:T(8,128)}, f32[3,512,256]{2,1,0:T(8,128)S(1)}, u32[]{:S(2)}) copy-start(f32[3,512,256]{2,1,0:T(8,128)S(1)} %slice_add_fusion) | copy-start | bytes 4718596
  181.6 7.1 %copy-start.1 = (f32[3,2,256,256]{3,2,0,1:T(8,128)S(1)}, f32[3,2,256,256]{3,2,0,1:T(8,128)}, u32[]{:S(2)}) copy-start(f32[3,2,256,256]{3,2,0,1:T(8,128)} %copy-done) | copy-start | bytes 4718596
  181.7 14.9 %collective-permute-start.3 = (f32[3,256,256]{2,1,0:T(8,128)S(1)}, f32[3,256,256]{2,1,0:T(8,128)S(1)}, u32[]{:S(2)}, u32[]{:S(2)}) collective-permute-start(f32[3,256,256]{2,1,0:T(8,128)S(1)} %slice.132), channel_id=1, source_target_pairs={{0,16},{16,32},{32,48},{48,64},{64,80},{80,96},{96,112},{112,128},... | collective-permute-start | bytes 2359304 | tf_op jit(solution)/shard_map/ppermute | solution.py:13
  189.6 478.6 %copy-start.3 = (f32[2,2,256,256]{3,2,1,0:T(8,128)S(1)}, f32[2,2,256,256]{3,2,1,0:T(8,128)}, u32[]{:S(2)}) copy-start(f32[2,2,256,256]{3,2,1,0:T(8,128)} %param.14) | copy-start | bytes 3145732
  189.6 480.9 %all-gather.3.cloned.1.call-start = ((), (), s32[]{:S(2)}) async-start(), calls=%async_computation | async-start | bytes 3932160 | tf_op jit(solution)/shard_map/all_gather | solution.py:98
  670.6 2.3 copy-start.6
Sparse Core Ops, SparseCore 0:
  189.8 477.4 all-reduce.2
Sparse Core Ops, SparseCore 1:
  198.8 58.4 all-gather.2
